TPU v7x, 32 devices: a whole 2x2x4 slice. The times are simulated.
32 devices in a mesh: pb: 8 (over z, y), pa: 4 (over x, core).
Axes of the slice: x: 2, y: 2, z: 4, core: 2. Of those that a mesh axis runs over, the one named last changes fastest.
Arguments:
- queries: float32 [8192, 4096], P('pb'), may hold values from -2.0898438 to 2.0898438
- passages: float32 [1024, 4096], P('pa', 'pb'), may hold values from -0.15625 to 0.15625
- pairs: int32 [96, 2], P('pb'), may hold values from 0 to 31, as said below
- positives: int32 [8192], P('pb'), may hold values from 0 to 1023, as said below
Outputs:
- losses: float32 [8192], P('pb')
- query_grad: float32 [8192, 4096], P('pb', 'pa')
- passage_grad: float32 [1024, 4096], P('pa', 'pb')
Inputs may be any that keep to these rules, and one draw needn't show every extreme that they name: Rows k * 12 to (k + 1) * 12 - 1 list query blocks k * 4 to (k + 1) * 4 - 1 only, in column 0; column 1 holds passage blocks. No pair appears twice and every query block appears in at least one pair; the number of pairs of a query block varies. The passage block of positives[i], positives[i] // 256, is listed with the query block of i.
All inputs are finite; a program needn't handle non-finite values.
Results may differ from a plain program's by a relative error of at most 0.0008.
Values sent between devices are 32-bit elements; how exact they have to be, the bound alone decides.
A program may use at most 192 MiB of HBM per device.

v0:
```python
import functools
import math

import jax
import jax.numpy as jnp
from jax import lax
from jax.experimental import pallas as pl
from jax.experimental.pallas import tpu as pltpu
from jax.sharding import PartitionSpec as P

BLK = 256
TILE = 256
low_value = -1e30
MESH = pl.DeviceIdType.MESH
F32 = jnp.float32
BF16 = jnp.bfloat16


def split(value):
    high = value.astype(BF16)
    return high, (value - high.astype(F32)).astype(BF16)


def dot3(left, right, dims):
    def one(a, b):
        return lax.dot_general(a, b, (dims, ((), ())), preferred_element_type=F32)

    return one(left[0], right[1]) + one(left[1], right[0]) + one(left[0], right[0])


def kernel(
    n_pb,
    n_pa,
    scale,
    q_hbm,
    p_hbm,
    pairs_ref,
    pos_ref,
    losses_ref,
    qgrad_hbm,
    pgrad_ref,
    qstage,
    qhi,
    qlo,
    feats,
    slab,
    scores,
    weights_in,
    stats,
    partial,
    y_up,
    y_down,
    near_in,
    z_up,
    z_down,
    qgrad,
    split_w,
    split_p,
    q_sem,
    own_sem,
    out_sem,
    feat_recv,
    zf_send,
    yf_send,
    near_send,
    slab_send,
    slab_recv,
    stat_send,
    stat_recv,
    w_send,
    w_pass,
    w_recv,
    yr_send,
    y_recv,
    near_out,
    near_recv,
    zr_send,
    z_recv,
):
    nx = n_pa // 2
    ny = nx
    nz = n_pb // ny
    ratio = n_pb // n_pa
    rows = q_hbm.shape[0]
    chunk = p_hbm.shape[1]
    group_rows = p_hbm.shape[0]
    half = group_rows // 2
    halves = [pl.ds(h * half, half) for h in range(2)]
    near = ny == 2 and nz >= 4
    q_blocks = rows // BLK
    p_blocks = group_rows // BLK

    me = lax.axis_index("pb")
    ga = lax.axis_index("pa")
    z = me // ny
    y = me % ny
    x = ga // 2
    core = ga % 2
    sibling = x * 2 + 1 - core

    def inside(value, size):
        return jnp.logical_and(value >= 0, value < size)

    def remote(src, dst, send_sem, recv_sem, **where):
        return pltpu.make_async_remote_copy(
            src_ref=src,
            dst_ref=dst,
            send_sem=send_sem,
            recv_sem=recv_sem,
            device_id=where,
            device_id_type=MESH,
        )

    def arrived(buffer, sem):
        remote(buffer, buffer, own_sem, sem, pa=sibling).wait_recv()

    def q_copy(k):
        start = pl.multiple_of(k * chunk, chunk)
        slot = lax.rem(k, 2)
        return pltpu.make_async_copy(
            q_hbm.at[:, pl.ds(start, chunk)], qstage.at[slot], q_sem.at[slot]
        )

    own_copy = pltpu.make_async_copy(p_hbm, feats.at[me], own_sem)
    own_copy.start()
    q_copy(jnp.int32(0)).start()
    q_copy(jnp.int32(1)).start()

    barrier = pltpu.get_barrier_semaphore()
    greeted = jnp.int32(n_pa - 1)
    for step in (1, -1):
        for valid, target in (
            (inside(z + step, nz), (z + step) * ny + y),
            (inside(y + step, ny), z * ny + y + step),
        ):

            @pl.when(valid)
            def _(target=target):
                pl.semaphore_signal(barrier, inc=1, device_id={"pb": target}, device_id_type=MESH)

            greeted = greeted + valid.astype(jnp.int32)
    for i in range(1, n_pa):
        pl.semaphore_signal(
            barrier, inc=1, device_id={"pa": lax.rem(ga + i, n_pa)}, device_id_type=MESH
        )
    pl.semaphore_wait(barrier, greeted)
    own_copy.wait()

    def feature(k, h, send_sem, **where):
        ref = feats.at[k, halves[h]]
        return remote(ref, ref, send_sem, feat_recv.at[k, h], **where)

    def z_feature(k, h, d):
        way = 0 if d > 0 else 1
        return feature(k, h, zf_send.at[way, k, h], pb=(z + d) * ny + y)

    def y_feature(k, h, e):
        way = 0 if e > 0 else 1
        return feature(k, h, yf_send.at[way, k, h], pb=z * ny + y + e)

    def near_feature(d):
        way = 0 if d > 0 else 1
        return feature(z * ny + 1 - y, 1, near_send.at[way], pb=(z + d) * ny + y)

    def feature_arrived(k, h):
        arrived(feats.at[k, halves[h]], feat_recv.at[k, h])

    def slab_feature(k):
        return remote(
            feats.at[k],
            slab.at[ga, k % ratio],
            slab_send.at[k],
            slab_recv.at[ga, k % ratio],
            pa=k // ratio,
        )

    def when_start(valid, make):
        @pl.when(valid)
        def _():
            make().start()

    def when_sent(valid, make):
        @pl.when(valid)
        def _():
            make().wait_send()

    for h in range(2):
        for d in (1, -1):
            when_start(inside(z + d, nz), lambda d=d: z_feature(me, h, d))
        for e in (1, -1):
            when_start(inside(y + e, ny), lambda e=e: y_feature(me, h, e))
    when_start(me // ratio != ga, lambda: slab_feature(me))

    @pl.loop(0, n_pb)
    def _(k):
        q_copy(k).wait()
        slot = lax.rem(k, 2)

        @pl.loop(0, rows // 128)
        def _(t):
            part = pl.ds(pl.multiple_of(t * 128, 128), 128)
            high, low = split(qstage[slot, part, :])
            qhi[k, part, :] = high
            qlo[k, part, :] = low

        @pl.when(k + 2 < n_pb)
        def _():
            q_copy(k + 2).start()

    scores[...] = jnp.zeros_like(scores)

    def add_scores(k):
        high, low = split(feats[k])

        @pl.loop(0, rows // TILE)
        def _(t):
            part = pl.ds(pl.multiple_of(t * TILE, TILE), TILE)
            scores[:, part] += dot3(
                (high, low), (qhi[k, part, :], qlo[k, part, :]), ((1,), (1,))
            )

    add_scores(me)

    def y_round(r):
        for d in (1, -1):
            zz = z + d * r
            once = inside(zz, nz) if d > 0 else jnp.logical_and(inside(zz, nz), r > 0)
            for t in range(1, ny):
                for e in (1, -1):
                    yy = y + e * t
                    k = zz * ny + yy

                    @pl.when(jnp.logical_and(once, inside(yy, ny)))
                    def _(k=k, e=e):
                        for h in range(2):
                            feature_arrived(k, h)
                            when_start(inside(y - e, ny), lambda: y_feature(k, h, -e))
                        when_start(k // ratio != ga, lambda: slab_feature(k))
                        add_scores(k)

    @pl.loop(1, nz)
    def _(s):
        for h in range(2):
            for d in (1, -1):
                zz = z + d * s
                k = zz * ny + y

                @pl.when(inside(zz, nz))
                def _(k=k, d=d, h=h):
                    feature_arrived(k, h)
                    when_start(inside(z - d, nz), lambda: z_feature(k, h, -d))
                    for e in (1, -1):
                        whole = s > 1 if near and h == 1 else True
                        when_start(
                            jnp.logical_and(whole, inside(y + e, ny)),
                            lambda e=e: y_feature(k, h, e),
                        )
                    if h == 1:
                        when_start(k // ratio != ga, lambda: slab_feature(k))

        if near:
            for d in (1, -1):
                when_start(
                    jnp.logical_and(s == nz - 2, inside(z + d, nz)), lambda d=d: near_feature(d)
                )

        for d in (1, -1):
            zz = z + d * s

            @pl.when(inside(zz, nz))
            def _(zz=zz):
                add_scores(zz * ny + y)

        @pl.when(s == 1)
        def _():
            y_round(jnp.int32(0))

    @pl.loop(0, nz - 1)
    def _(i):
        y_round(jnp.where(i < nz - 2, i + 2, 1))

    q_first = me * q_blocks
    lane_block = lax.broadcasted_iota(jnp.int32, (1, rows), 1) // BLK

    def live_lanes(p_block):
        same = jnp.logical_and(
            pairs_ref[:, 0:1] - q_first == lane_block,
            pairs_ref[:, 1:2] == ga * p_blocks + p_block,
        )
        return jnp.max(same.astype(jnp.int32), axis=0, keepdims=True) > 0

    live = [live_lanes(b) for b in range(p_blocks)]
    row_ids = lax.broadcasted_iota(jnp.int32, (BLK, rows), 0)

    def positive_mask(b):
        return row_ids == pos_ref[...] - (ga * p_blocks + b) * BLK

    tops, totals, hits = [], [], []
    for b in range(p_blocks):
        tile = scores[b * BLK : (b + 1) * BLK, :] * scale
        scores[b * BLK : (b + 1) * BLK, :] = tile
        top = jnp.max(tile, axis=0, keepdims=True)
        total = jnp.sum(jnp.exp(tile - top), axis=0, keepdims=True)
        tops.append(jnp.where(live[b], top, low_value))
        totals.append(jnp.where(live[b], total, 0.0))
        hits.append(jnp.sum(jnp.where(positive_mask(b), tile, 0.0), axis=0, keepdims=True))

    def merge(tops, totals):
        joint = functools.reduce(jnp.maximum, tops)
        return joint, sum(t * jnp.exp(m - joint) for m, t in zip(tops, totals))

    top, total = merge(tops, totals)
    stats[ga, 0:1, :] = top
    stats[ga, 1:2, :] = total
    stats[ga, 2:3, :] = sum(hits)
    stats[ga, 3:8, :] = jnp.zeros((5, rows), F32)

    def stat_copy(i):
        return remote(
            stats.at[ga],
            stats.at[ga],
            stat_send.at[i - 1],
            stat_recv.at[ga],
            pa=lax.rem(ga + i, n_pa),
        )

    for i in range(1, n_pa):
        stat_copy(i).start()
    for i in range(1, n_pa):
        other = lax.rem(ga + i, n_pa)
        arrived(stats.at[other], stat_recv.at[other])
    joint, total = merge(
        [stats[g, 0:1, :] for g in range(n_pa)], [stats[g, 1:2, :] for g in range(n_pa)]
    )
    log_norm = joint + jnp.log(total)
    losses_ref[...] = log_norm - sum(stats[g, 2:3, :] for g in range(n_pa))

    for b in range(p_blocks):
        tile = scores[b * BLK : (b + 1) * BLK, :]
        soft = jnp.where(live[b], jnp.exp(tile - log_norm), 0.0)
        weight = soft - positive_mask(b).astype(F32)
        scores[b * BLK : (b + 1) * BLK, :] = weight
        high, low = split(weight)
        split_w[0, b * BLK : (b + 1) * BLK, :] = high
        split_w[1, b * BLK : (b + 1) * BLK, :] = low

    def w_copy(i):
        target = lax.rem(x + i, nx) * 2 + core if i else sibling
        return remote(scores, weights_in.at[ga], w_send.at[i], w_recv.at[ga], pa=target)

    def w_forward(i):
        g = lax.rem(x + i, nx) * 2 + core
        return remote(weights_in.at[g], weights_in.at[g], w_pass.at[i], w_recv.at[g], pa=sibling)

    for i in range(nx):
        w_copy(i).start()

    def form_partial(k):
        left = (split_w[0], split_w[1])
        for n in range(0, chunk, TILE):
            part = pl.ds(n, TILE)
            partial[k, :, part] = scale * dot3(
                left, (qhi[k, :, part], qlo[k, :, part]), ((1,), (0,))
            )

    def y_slot(zz, yy, e, h):
        return y_up.at[zz, yy - 1, halves[h]] if e > 0 else y_down.at[zz, yy, halves[h]]

    def y_sem(zz, yy, e, h):
        return y_recv.at[0 if e > 0 else 1, zz, yy - 1 if e > 0 else yy, h]

    def add_partial(k, h, slot, sem):
        arrived(slot, sem)
        partial[k, halves[h]] += slot[...]

    def y_sum(zz, yy, e, h):
        add_partial(zz * ny + yy, h, y_slot(zz, yy, e, h), y_sem(zz, yy, e, h))

    def y_partial(zz, yy, e, h):
        way = 0 if e > 0 else 1
        k = zz * ny + yy
        return remote(
            partial.at[k, halves[h]],
            y_slot(zz, yy, e, h),
            yr_send.at[way, k, h],
            y_sem(zz, yy, e, h),
            pb=z * ny + y + e,
        )

    def near_partial(d):
        way = 0 if d > 0 else 1
        return remote(
            partial.at[(z + d) * ny + 1 - y, halves[1]],
            near_in.at[way],
            near_out.at[way],
            near_recv.at[way],
            pb=(z + d) * ny + y,
        )

    def each_z(body, last):
        @pl.loop(0, nz - last)
        def _(i):
            s = nz - 1 - i
            for d in (1, -1):
                zz = z + d * s
                valid = inside(zz, nz) if d > 0 else jnp.logical_and(inside(zz, nz), s > 0)

                @pl.when(valid)
                def _(zz=zz, d=d):
                    body(zz, d, s)

    for t in range(ny - 1, 0, -1):
        for e in (1, -1):
            yy = y + e * t

            @pl.when(inside(yy, ny))
            def _(yy=yy, e=e):
                def send_one(zz, d, s):
                    form_partial(zz * ny + yy)
                    for h in range(2):

                        @pl.when(inside(y - e, ny))
                        def _(h=h):
                            y_sum(zz, yy, e, h)

                        direct = s > 1 if near and h == 1 else True
                        when_start(direct, lambda: y_partial(zz, yy, e, h))
                    if near:
                        when_start(s == 1, lambda: near_partial(d))

                each_z(send_one, 0)

    each_z(lambda zz, d, s: form_partial(zz * ny + y), 0)

    if near:
        across = z * ny + 1 - y
        for d in (1, -1):
            way = 0 if d > 0 else 1

            @pl.when(inside(z - d, nz))
            def _(way=way):
                add_partial(across, 1, near_in.at[way], near_recv.at[way])

        for e in (1, -1):
            when_start(inside(y + e, ny), lambda e=e: y_partial(z, y + e, e, 1))

    def z_slot(zz, d, h):
        return z_up.at[zz - 1, halves[h]] if d > 0 else z_down.at[zz, halves[h]]

    def z_sem(zz, d, h):
        return z_recv.at[0 if d > 0 else 1, zz - 1 if d > 0 else zz, h]

    def z_partial(zz, d, h):
        way = 0 if d > 0 else 1
        return remote(
            partial.at[zz * ny + y, halves[h]],
            z_slot(zz, d, h),
            zr_send.at[way, zz, h],
            z_sem(zz, d, h),
            pb=(z + d) * ny + y,
        )

    def y_gather(zz, h):
        for e in (1, -1):

            @pl.when(inside(y - e, ny))
            def _(e=e):
                y_sum(zz, y, e, h)

    def z_sum(zz, d, h):
        add_partial(zz * ny + y, h, z_slot(zz, d, h), z_sem(zz, d, h))

    def z_step(s):
        for h in range(2):
            for d in (1, -1):
                zz = z + d * s

                @pl.when(inside(zz, nz))
                def _(zz=zz, d=d, h=h):
                    if not (near and s == 1 and h == 1):
                        y_gather(zz, h)

                    @pl.when(inside(z - d, nz))
                    def _():
                        z_sum(zz, d, h)

                    z_partial(zz, d, h).start()

    def add_query_grad(w_ref, p_refs, first):
        for j in range(ratio):
            high, low = split(p_refs[j][...])
            split_p[j, 0] = high
            split_p[j, 1] = low

        @pl.loop(0, rows // TILE)
        def _(t):
            part = pl.ds(pl.multiple_of(t * TILE, TILE), TILE)
            left = split(w_ref[:, part].T)
            for j in range(ratio):
                cols = pl.ds(j * chunk, chunk)
                term = scale * dot3(left, (split_p[j, 0], split_p[j, 1]), ((1,), (0,)))
                if first:
                    qgrad[part, cols] = term
                else:
                    qgrad[part, cols] += term

    def group_query_grad(g):
        arrived(weights_in.at[g], w_recv.at[g])
        wait_slab(g)
        add_query_grad(weights_in.at[g], [slab.at[g, j] for j in range(ratio)], False)

    def wait_slab(g):
        for j in range(ratio):
            arrived(slab.at[g, j], slab_recv.at[g, j])

    def same_core_query_grad(i):
        g = lax.rem(x + i, nx) * 2 + core
        wait_slab(g)
        add_query_grad(weights_in.at[g], [slab.at[g, j] for j in range(ratio)], False)

    add_query_grad(scores, [feats.at[ga * ratio + j] for j in range(ratio)], True)
    z_step(nz - 1)
    group_query_grad(sibling)
    for s in range(nz - 2, 0, -1):
        z_step(s)
    for i in range(1, nx):
        g = lax.rem(x + i, nx) * 2 + core
        arrived(weights_in.at[g], w_recv.at[g])
        w_forward(i).start()
    for i in range(1, nx):
        same_core_query_grad(i)
    for i in range(1, nx):
        group_query_grad(lax.rem(x + i, nx) * 2 + 1 - core)
    out_copy = pltpu.make_async_copy(qgrad, qgrad_hbm, out_sem)
    out_copy.start()

    for h in range(2):
        for d in (1, -1):

            @pl.when(inside(z - d, nz))
            def _(d=d, h=h):
                z_sum(z, d, h)

        y_gather(z, h)

    pgrad_ref[...] = partial[me]

    @pl.loop(0, n_pb)
    def _(k):
        zz = k // ny
        yy = k % ny
        when_sent(k // ratio != ga, lambda: slab_feature(k))
        for h in range(2):
            far = jnp.abs(zz - z) != 1 if near and h == 1 else True
            for d in (1, -1):
                behind = zz <= z if d > 0 else zz >= z
                ahead = zz > z if d > 0 else zz < z
                line = yy == y
                when_sent(
                    jnp.logical_and(jnp.logical_and(line, behind), inside(z + d, nz)),
                    lambda d=d: z_feature(k, h, d),
                )
                when_sent(jnp.logical_and(line, ahead), lambda d=d: z_partial(zz, d, h))
            for e in (1, -1):
                behind = yy <= y if e > 0 else yy >= y
                ahead = yy > y if e > 0 else yy < y
                when_sent(
                    jnp.logical_and(far, jnp.logical_and(behind, inside(y + e, ny))),
                    lambda e=e: y_feature(k, h, e),
                )
                when_sent(jnp.logical_and(far, ahead), lambda e=e: y_partial(zz, yy, e, h))

    if near:
        for d in (1, -1):
            when_sent(inside(z + d, nz), lambda d=d: near_feature(d))
            when_sent(inside(z + d, nz), lambda d=d: near_partial(d))
    for i in range(1, n_pa):
        stat_copy(i).wait_send()
    for i in range(nx):
        w_copy(i).wait_send()
    for i in range(1, nx):
        w_forward(i).wait_send()
    out_copy.wait()


def body(n_pb, n_pa, queries, passages, pairs, positives):
    rows, width = queries.shape
    group_rows, chunk = passages.shape
    nx = n_pa // 2
    ny = nx
    nz = n_pb // ny
    ratio = n_pb // n_pa
    dma = pltpu.SemaphoreType.DMA
    losses, query_grad, passage_grad = pl.pallas_call(
        functools.partial(kernel, n_pb, n_pa, math.sqrt(width)),
        out_shape=(
            jax.ShapeDtypeStruct((1, rows), F32),
            jax.ShapeDtypeStruct((rows, ratio * chunk), F32),
            jax.ShapeDtypeStruct((group_rows, chunk), F32),
        ),
        in_specs=[
            pl.BlockSpec(memory_space=pl.ANY),
            pl.BlockSpec(memory_space=pl.ANY),
            pl.BlockSpec(memory_space=pltpu.VMEM),
            pl.BlockSpec(memory_space=pltpu.VMEM),
        ],
        out_specs=(
            pl.BlockSpec(memory_space=pltpu.VMEM),
            pl.BlockSpec(memory_space=pl.ANY),
            pl.BlockSpec(memory_space=pltpu.VMEM),
        ),
        scratch_shapes=[
            pltpu.VMEM((2, rows, chunk), F32),
            pltpu.VMEM((n_pb, rows, chunk), BF16),
            pltpu.VMEM((n_pb, rows, chunk), BF16),
            pltpu.VMEM((n_pb, group_rows, chunk), F32),
            pltpu.VMEM((n_pa, ratio, group_rows, chunk), F32),
            pltpu.VMEM((group_rows, rows), F32),
            pltpu.VMEM((n_pa, group_rows, rows), F32),
            pltpu.VMEM((n_pa, 8, rows), F32),
            pltpu.VMEM((n_pb, group_rows, chunk), F32),
            pltpu.VMEM((nz, ny - 1, group_rows, chunk), F32),
            pltpu.VMEM((nz, ny - 1, group_rows, chunk), F32),
            pltpu.VMEM((2, group_rows // 2, chunk), F32),
            pltpu.VMEM((nz - 1, group_rows, chunk), F32),
            pltpu.VMEM((nz - 1, group_rows, chunk), F32),
            pltpu.VMEM((rows, ratio * chunk), F32),
            pltpu.VMEM((2, group_rows, rows), BF16),
            pltpu.VMEM((ratio, 2, group_rows, chunk), BF16),
            dma((2,)),
            dma,
            dma,
            dma((n_pb, 2)),
            dma((2, n_pb, 2)),
            dma((2, n_pb, 2)),
            dma((2,)),
            dma((n_pb,)),
            dma((n_pa, ratio)),
            dma((n_pa - 1,)),
            dma((n_pa,)),
            dma((nx,)),
            dma((nx,)),
            dma((n_pa,)),
            dma((2, n_pb, 2)),
            dma((2, nz, ny - 1, 2)),
            dma((2,)),
            dma((2,)),
            dma((2, nz, 2)),
            dma((2, nz - 1, 2)),
        ],
        compiler_params=pltpu.CompilerParams(
            collective_id=0, has_side_effects=True, vmem_limit_bytes=62 * 2**20
        ),
    )(queries, passages, pairs, positives.reshape(1, rows))
    return losses.reshape(-1), query_grad, passage_grad


def solution(mesh):
    in_specs = (P("pb", None), P("pa", "pb"), P("pb", None), P("pb"))
    out_specs = (P("pb"), P("pb", "pa"), P("pa", "pb"))
    return jax.shard_map(
        functools.partial(body, mesh.shape["pb"], mesh.shape["pa"]),
        mesh=mesh,
        in_specs=in_specs,
        out_specs=out_specs,
        check_vma=False,
    )
```

profile of v0, /device:TPU:16, one launch (start us, length us, event | category | flops | bytes accessed | tf_op | source)
XLA Modules:
  0.0 135.5 jit_solution(11373340014420324594)
XLA Ops:
  0.6 1.4 %copy.7.pairs_ref = s32[12,2]{1,0:T(8,128)} copy(s32[12,2]{0,1:T(2,128)} %param.6) | data formatting | bytes 192 | tf_op args[2]
  2.0 126.6 %shard_map.67 = (f32[1,1024]{1,0:T(1,128)}, f32[1024,1024]{1,0:T(8,128)}, f32[256,512]{1,0:T(8,128)}) custom-call(f32[1024,4096]{1,0:T(8,128)} %q_hbm.1, f32[256,512]{1,0:T(8,128)} %p_hbm.1, s32[12,2]{1,0:T(8,128)} %copy.7.pairs_ref, s32[1,1024]{1,0:T(1,128)} %bitcast.2), custom_call_target="tpu_custom_call" | custom-call | tf_op jit(solution)/shard_map/pallas_call | solution.py:594
  128.6 1.3 copy.11
  129.9 0.0 copy-start
  129.9 4.8 %copy.12 = f32[1024,1024]{1,0:T(8,128)} copy(f32[1024,1024]{1,0:T(8,128)} %get-tuple-element.13) | data formatting | bytes 8388608
  134.7 0.0 copy-done
  134.7 0.8 copy.13
Async XLA Ops:
  129.9 4.8 %copy-start = (f32[256,512]{1,0:T(8,128)S(1)}, f32[256,512]{1,0:T(8,128)}, u32[]{:S(2)}) copy-start(f32[256,512]{1,0:T(8,128)} %get-tuple-element.14) | copy-start | bytes 1572868
where the time goes:
time: 136 us
  Pallas kernels  127 us (93%)
  local copies, waits for them, and re-layouts  8.27 us (6%)
    pallas_call x1, Pallas kernels, body(): pl.pallas_call(functools.partial(kernel, n_pb, n_pa, math.sqrt(width)), o...  127 us
    unnamed x6, local copies, waits for them, and re-layouts  8.27 us

commit v1 on v0

--- a/solution.py
+++ b/solution.py
@@ -184,11 +184,13 @@
         def _():
             make().wait_send()
 
-    for h in range(2):
+    def send_own(h):
         for d in (1, -1):
             when_start(inside(z + d, nz), lambda d=d: z_feature(me, h, d))
         for e in (1, -1):
             when_start(inside(y + e, ny), lambda e=e: y_feature(me, h, e))
+
+    send_own(0)
     when_start(me // ratio != ga, lambda: slab_feature(me))
 
     @pl.loop(0, n_pb)
@@ -206,6 +208,10 @@
         @pl.when(k + 2 < n_pb)
         def _():
             q_copy(k + 2).start()
+
+        @pl.when(k == n_pb // 2)
+        def _():
+            send_own(1)
 
     scores[...] = jnp.zeros_like(scores)
 
@@ -409,40 +415,75 @@
                 def _(zz=zz, d=d):
                     body(zz, d, s)
 
-    for t in range(ny - 1, 0, -1):
-        for e in (1, -1):
-            yy = y + e * t
-
-            @pl.when(inside(yy, ny))
-            def _(yy=yy, e=e):
-                def send_one(zz, d, s):
-                    form_partial(zz * ny + yy)
-                    for h in range(2):
-
-                        @pl.when(inside(y - e, ny))
-                        def _(h=h):
-                            y_sum(zz, yy, e, h)
-
-                        direct = s > 1 if near and h == 1 else True
-                        when_start(direct, lambda: y_partial(zz, yy, e, h))
-                    if near:
-                        when_start(s == 1, lambda: near_partial(d))
-
-                each_z(send_one, 0)
+    across = 1 - y
+    farthest = jnp.maximum(z, nz - 1 - z)
+
+    def across_each(s, act):
+        for d in (1, -1) if not (isinstance(s, int) and s == 0) else (1,):
+            for e in (1, -1):
+                zz = z + d * s
+
+                @pl.when(jnp.logical_and(inside(zz, nz), inside(y + e, ny)))
+                def _(zz=zz, e=e):
+                    act(zz, e)
+
+    def across_start(s, h):
+        across_each(s, lambda zz, e: y_partial(zz, across, e, h).start())
+
+    def across_sent(s, h):
+        across_each(s, lambda zz, e: y_partial(zz, across, e, h).wait_send())
+
+    if near:
+        def form_across(zz, d, s):
+            form_partial(zz * ny + across)
+            when_start(s == 1, lambda: near_partial(d))
+
+            @pl.when(s == farthest)
+            def _():
+                for e in (1, -1):
+                    when_start(inside(y + e, ny), lambda e=e: y_partial(zz, across, e, 0))
+
+        each_z(form_across, 0)
+        across_start(farthest, 1)
+    else:
+        for t in range(ny - 1, 0, -1):
+            for e in (1, -1):
+                yy = y + e * t
+
+                @pl.when(inside(yy, ny))
+                def _(yy=yy, e=e):
+                    def send_one(zz, d, s):
+                        form_partial(zz * ny + yy)
+                        for h in range(2):
+
+                            @pl.when(inside(y - e, ny))
+                            def _(h=h):
+                                y_sum(zz, yy, e, h)
+
+                            y_partial(zz, yy, e, h).start()
+
+                    each_z(send_one, 0)
 
     each_z(lambda zz, d, s: form_partial(zz * ny + y), 0)
 
-    if near:
-        across = z * ny + 1 - y
-        for d in (1, -1):
-            way = 0 if d > 0 else 1
-
-            @pl.when(inside(z - d, nz))
-            def _(way=way):
-                add_partial(across, 1, near_in.at[way], near_recv.at[way])
-
-        for e in (1, -1):
-            when_start(inside(y + e, ny), lambda e=e: y_partial(z, y + e, e, 1))
+    def across_next(s, h):
+        if s > 1 or h == 0:
+
+            @pl.when(farthest >= s)
+            def _():
+                across_sent(s, h)
+                if s > 2 or h == 0:
+                    across_start(s - 1, h)
+
+        if s == 1 and h == 1:
+            for d in (1, -1):
+                way = 0 if d > 0 else 1
+
+                @pl.when(inside(z - d, nz))
+                def _(way=way):
+                    add_partial(z * ny + across, 1, near_in.at[way], near_recv.at[way])
+
+            across_start(0, 1)
 
     def z_slot(zz, d, h):
         return z_up.at[zz - 1, halves[h]] if d > 0 else z_down.at[zz, halves[h]]
@@ -472,6 +513,8 @@
 
     def z_step(s):
         for h in range(2):
+            if near:
+                across_next(s, h)
             for d in (1, -1):
                 zz = z + d * s
 
@@ -518,8 +561,8 @@
         wait_slab(g)
         add_query_grad(weights_in.at[g], [slab.at[g, j] for j in range(ratio)], False)
 
+    z_step(nz - 1)
     add_query_grad(scores, [feats.at[ga * ratio + j] for j in range(ratio)], True)
-    z_step(nz - 1)
     group_query_grad(sibling)
     for s in range(nz - 2, 0, -1):
         z_step(s)
@@ -552,6 +595,7 @@
         when_sent(k // ratio != ga, lambda: slab_feature(k))
         for h in range(2):
             far = jnp.abs(zz - z) != 1 if near and h == 1 else True
+            unsent = zz == z if near else True
             for d in (1, -1):
                 behind = zz <= z if d > 0 else zz >= z
                 ahead = zz > z if d > 0 else zz < z
@@ -568,7 +612,7 @@
                     jnp.logical_and(far, jnp.logical_and(behind, inside(y + e, ny))),
                     lambda e=e: y_feature(k, h, e),
                 )
-                when_sent(jnp.logical_and(far, ahead), lambda e=e: y_partial(zz, yy, e, h))
+                when_sent(jnp.logical_and(unsent, ahead), lambda e=e: y_partial(zz, yy, e, h))
 
     if near:
         for d in (1, -1):

time: 136 us -> 134 us (0.985)
  Pallas kernels: 127 us -> 125 us
    pallas_call x1, Pallas kernels: 127 us -> 125 us  [body(): pl.pallas_call(functools.partial(kernel, n_pb, n_pa, math.sqrt(width)), o...]
where the time goes in v1:
time: 134 us
  Pallas kernels  125 us (93%)
  local copies, waits for them, and re-layouts  8.27 us (6%)
    pallas_call x1, Pallas kernels, body(): pl.pallas_call(functools.partial(kernel, n_pb, n_pa, math.sqrt(width)), o...  125 us
    unnamed x6, local copies, waits for them, and re-layouts  8.27 us

profile of v1, /device:TPU:16, one launch (start us, length us, event | category | flops | bytes accessed | tf_op | source)
XLA Modules:
  0.0 133.6 jit_solution(8765974045705080739)
XLA Ops:
  0.6 1.4 %copy.7.pairs_ref = s32[12,2]{1,0:T(8,128)} copy(s32[12,2]{0,1:T(2,128)} %param.6) | data formatting | bytes 192 | tf_op args[2]
  2.0 124.7 %shard_map.67 = (f32[1,1024]{1,0:T(1,128)}, f32[1024,1024]{1,0:T(8,128)}, f32[256,512]{1,0:T(8,128)}) custom-call(f32[1024,4096]{1,0:T(8,128)} %q_hbm.1, f32[256,512]{1,0:T(8,128)} %p_hbm.1, s32[12,2]{1,0:T(8,128)} %copy.7.pairs_ref, s32[1,1024]{1,0:T(1,128)} %bitcast.2), custom_call_target="tpu_custom_call" | custom-call | tf_op jit(solution)/shard_map/pallas_call | solution.py:638
  126.7 1.3 copy.11
  128.0 0.0 copy-start
  128.0 4.8 %copy.12 = f32[1024,1024]{1,0:T(8,128)} copy(f32[1024,1024]{1,0:T(8,128)} %get-tuple-element.13) | data formatting | bytes 8388608
  132.8 0.0 copy-done
  132.8 0.8 copy.13
Async XLA Ops:
  128.0 4.8 %copy-start = (f32[256,512]{1,0:T(8,128)S(1)}, f32[256,512]{1,0:T(8,128)}, u32[]{:S(2)}) copy-start(f32[256,512]{1,0:T(8,128)} %get-tuple-element.14) | copy-start | bytes 1572868

commit v2 on v1

--- a/solution.py
+++ b/solution.py
@@ -39,6 +39,8 @@
     losses_ref,
     qgrad_hbm,
     pgrad_ref,
+    w_out,
+    slab_out,
     qstage,
     qhi,
     qlo,
@@ -165,12 +167,12 @@
     def feature_arrived(k, h):
         arrived(feats.at[k, halves[h]], feat_recv.at[k, h])
 
-    def slab_feature(k):
+    def slab_feature(k, h):
         return remote(
-            feats.at[k],
-            slab.at[ga, k % ratio],
-            slab_send.at[k],
-            slab_recv.at[ga, k % ratio],
+            feats.at[k, halves[h]],
+            slab.at[ga, k % ratio, halves[h]],
+            slab_send.at[k, h],
+            slab_recv.at[ga, k % ratio, h],
             pa=k // ratio,
         )
 
@@ -191,7 +193,8 @@
             when_start(inside(y + e, ny), lambda e=e: y_feature(me, h, e))
 
     send_own(0)
-    when_start(me // ratio != ga, lambda: slab_feature(me))
+    for h in range(2):
+        when_start(me // ratio != ga, lambda: slab_feature(me, h))
 
     @pl.loop(0, n_pb)
     def _(k):
@@ -227,7 +230,7 @@
 
     add_scores(me)
 
-    def y_round(r):
+    def y_round(r, parts, score):
         for d in (1, -1):
             zz = z + d * r
             once = inside(zz, nz) if d > 0 else jnp.logical_and(inside(zz, nz), r > 0)
@@ -238,11 +241,12 @@
 
                     @pl.when(jnp.logical_and(once, inside(yy, ny)))
                     def _(k=k, e=e):
-                        for h in range(2):
+                        for h in parts:
                             feature_arrived(k, h)
                             when_start(inside(y - e, ny), lambda: y_feature(k, h, -e))
-                        when_start(k // ratio != ga, lambda: slab_feature(k))
-                        add_scores(k)
+                            when_start(k // ratio != ga, lambda: slab_feature(k, h))
+                        if score:
+                            add_scores(k)
 
     @pl.loop(1, nz)
     def _(s):
@@ -261,8 +265,7 @@
                             jnp.logical_and(whole, inside(y + e, ny)),
                             lambda e=e: y_feature(k, h, e),
                         )
-                    if h == 1:
-                        when_start(k // ratio != ga, lambda: slab_feature(k))
+                    when_start(k // ratio != ga, lambda: slab_feature(k, h))
 
         if near:
             for d in (1, -1):
@@ -279,21 +282,30 @@
 
         @pl.when(s == 1)
         def _():
-            y_round(jnp.int32(0))
+            y_round(jnp.int32(0), (0, 1), True)
+
+        @pl.when(s > 1)
+        def _():
+            y_round(s - 1, (0,), False)
+
+    y_round(nz - 1, (0,), False)
 
     @pl.loop(0, nz - 1)
     def _(i):
-        y_round(jnp.where(i < nz - 2, i + 2, 1))
+        y_round(jnp.where(i < nz - 2, i + 2, 1), (1,), True)
 
     q_first = me * q_blocks
     lane_block = lax.broadcasted_iota(jnp.int32, (1, rows), 1) // BLK
 
     def live_lanes(p_block):
-        same = jnp.logical_and(
-            pairs_ref[:, 0:1] - q_first == lane_block,
-            pairs_ref[:, 1:2] == ga * p_blocks + p_block,
-        )
-        return jnp.max(same.astype(jnp.int32), axis=0, keepdims=True) > 0
+        found = jnp.zeros((1, rows), jnp.int32)
+        for r in range(pairs_ref.shape[1]):
+            same = jnp.logical_and(
+                pairs_ref[0:1, r : r + 1] - q_first == lane_block,
+                pairs_ref[1:2, r : r + 1] == ga * p_blocks + p_block,
+            )
+            found = found + same.astype(jnp.int32)
+        return found > 0
 
     live = [live_lanes(b) for b in range(p_blocks)]
     row_ids = lax.broadcasted_iota(jnp.int32, (BLK, rows), 0)
@@ -554,7 +566,8 @@
 
     def wait_slab(g):
         for j in range(ratio):
-            arrived(slab.at[g, j], slab_recv.at[g, j])
+            for h in range(2):
+                arrived(slab.at[g, j, halves[h]], slab_recv.at[g, j, h])
 
     def same_core_query_grad(i):
         g = lax.rem(x + i, nx) * 2 + core
@@ -572,10 +585,18 @@
         w_forward(i).start()
     for i in range(1, nx):
         same_core_query_grad(i)
-    for i in range(1, nx):
+    for i in range(1, nx - 1):
         group_query_grad(lax.rem(x + i, nx) * 2 + 1 - core)
-    out_copy = pltpu.make_async_copy(qgrad, qgrad_hbm, out_sem)
+    out_copy = pltpu.make_async_copy(qgrad, qgrad_hbm, out_sem.at[0])
     out_copy.start()
+
+    last = lax.rem(x + nx - 1, nx) * 2 + 1 - core
+    arrived(weights_in.at[last], w_recv.at[last])
+    w_out_copy = pltpu.make_async_copy(weights_in.at[last], w_out, out_sem.at[1])
+    w_out_copy.start()
+    wait_slab(last)
+    slab_out_copy = pltpu.make_async_copy(slab.at[last], slab_out, out_sem.at[2])
+    slab_out_copy.start()
 
     for h in range(2):
         for d in (1, -1):
@@ -592,7 +613,8 @@
     def _(k):
         zz = k // ny
         yy = k % ny
-        when_sent(k // ratio != ga, lambda: slab_feature(k))
+        for h in range(2):
+            when_sent(k // ratio != ga, lambda: slab_feature(k, h))
         for h in range(2):
             far = jnp.abs(zz - z) != 1 if near and h == 1 else True
             unsent = zz == z if near else True
@@ -625,6 +647,25 @@
     for i in range(1, nx):
         w_forward(i).wait_send()
     out_copy.wait()
+    w_out_copy.wait()
+    slab_out_copy.wait()
+
+
+def last_kernel(scale, so_far, weights, slab, out, split_p):
+    ratio, _, chunk = slab.shape
+
+    @pl.when(pl.program_id(0) == 0)
+    def _():
+        for j in range(ratio):
+            high, low = split(slab[j])
+            split_p[j, 0] = high
+            split_p[j, 1] = low
+
+    left = split(weights[...].T)
+    for j in range(ratio):
+        cols = pl.ds(j * chunk, chunk)
+        term = dot3(left, (split_p[j, 0], split_p[j, 1]), ((1,), (0,)))
+        out[:, cols] = so_far[:, cols] + scale * term
 
 
 def body(n_pb, n_pa, queries, passages, pairs, positives):
@@ -635,12 +676,14 @@
     nz = n_pb // ny
     ratio = n_pb // n_pa
     dma = pltpu.SemaphoreType.DMA
-    losses, query_grad, passage_grad = pl.pallas_call(
+    losses, most, passage_grad, weights, slab = pl.pallas_call(
         functools.partial(kernel, n_pb, n_pa, math.sqrt(width)),
         out_shape=(
             jax.ShapeDtypeStruct((1, rows), F32),
             jax.ShapeDtypeStruct((rows, ratio * chunk), F32),
             jax.ShapeDtypeStruct((group_rows, chunk), F32),
+            jax.ShapeDtypeStruct((group_rows, rows), F32),
+            jax.ShapeDtypeStruct((ratio, group_rows, chunk), F32),
         ),
         in_specs=[
             pl.BlockSpec(memory_space=pl.ANY),
@@ -652,6 +695,8 @@
             pl.BlockSpec(memory_space=pltpu.VMEM),
             pl.BlockSpec(memory_space=pl.ANY),
             pl.BlockSpec(memory_space=pltpu.VMEM),
+            pl.BlockSpec(memory_space=pl.ANY),
+            pl.BlockSpec(memory_space=pl.ANY),
         ),
         scratch_shapes=[
             pltpu.VMEM((2, rows, chunk), F32),
@@ -673,13 +718,13 @@
             pltpu.VMEM((ratio, 2, group_rows, chunk), BF16),
             dma((2,)),
             dma,
-            dma,
+            dma((3,)),
             dma((n_pb, 2)),
             dma((2, n_pb, 2)),
             dma((2, n_pb, 2)),
             dma((2,)),
-            dma((n_pb,)),
-            dma((n_pa, ratio)),
+            dma((n_pb, 2)),
+            dma((n_pa, ratio, 2)),
             dma((n_pa - 1,)),
             dma((n_pa,)),
             dma((nx,)),
@@ -695,7 +740,21 @@
         compiler_params=pltpu.CompilerParams(
             collective_id=0, has_side_effects=True, vmem_limit_bytes=62 * 2**20
         ),
-    )(queries, passages, pairs, positives.reshape(1, rows))
+    )(queries, passages, pairs.T, positives.reshape(1, rows))
+    tile_spec = pl.BlockSpec((TILE, ratio * chunk), lambda t: (t, 0))
+    query_grad = pl.pallas_call(
+        functools.partial(last_kernel, math.sqrt(width)),
+        grid=(rows // TILE,),
+        out_shape=jax.ShapeDtypeStruct((rows, ratio * chunk), F32),
+        in_specs=[
+            tile_spec,
+            pl.BlockSpec((group_rows, TILE), lambda t: (0, t)),
+            pl.BlockSpec((ratio, group_rows, chunk), lambda t: (0, 0, 0)),
+        ],
+        out_specs=tile_spec,
+        scratch_shapes=[pltpu.VMEM((ratio, 2, group_rows, chunk), BF16)],
+        compiler_params=pltpu.CompilerParams(vmem_limit_bytes=62 * 2**20),
+    )(most, weights, slab)
     return losses.reshape(-1), query_grad, passage_grad
 
 

time: 134 us -> 128 us (0.955)
  local copies, waits for them, and re-layouts: 8.27 us -> 1.4 us
    unnamed x6, local copies, waits for them, and re-layouts: 8.27 us -> 1.4 us
    pallas_call x0 -> x1, Pallas kernels: none -> 6.72 us  [body(): pl.pallas_call(functools.partial(last_kernel, math.sqrt(width)), grid=(ro...]
    pallas_call x1, Pallas kernels: 125 us -> 119 us  [body(): pl.pallas_call(functools.partial(kernel, n_pb, n_pa, math.sqrt(width)), o...]
where the time goes in v2:
time: 128 us
  Pallas kernels  126 us (98%)
  local copies, waits for them, and re-layouts  1.4 us (1%)
    pallas_call x1, Pallas kernels, body(): pl.pallas_call(functools.partial(kernel, n_pb, n_pa, math.sqrt(width)), o...  119 us
    pallas_call x1, Pallas kernels, body(): pl.pallas_call(functools.partial(last_kernel, math.sqrt(width)), grid=(ro...  6.72 us

profile of v2, /device:TPU:16, one launch (start us, length us, event | category | flops | bytes accessed | tf_op | source)
XLA Modules:
  0.0 128.0 jit_solution(14772483897835101830)
XLA Ops:
  0.6 119.3 %shard_map.67 = (f32[1,1024]{1,0:T(1,128)}, f32[1024,1024]{1,0:T(8,128)}, f32[256,512]{1,0:T(8,128)}, f32[256,1024]{1,0:T(8,128)}, f32[2,256,512]{2,1,0:T(8,128)}) custom-call(f32[1024,4096]{1,0:T(8,128)} %q_hbm.1, f32[256,512]{1,0:T(8,128)} %p_hbm.1, s32[2,12]{1,0:T(2,128)} %bitcast.5, s32[1,1024]{1,0:T(1,128)} %bitcast.3), custom_call_target="tpu_custom_call" | custom-call | tf_op jit(solution)/shard_map/pallas_call | solution.py:679
  119.9 0.0 copy-start.1
  119.9 0.0 copy-start
  119.9 6.7 %shard_map.68 = f32[1024,1024]{1,0:T(8,128)} custom-call(f32[1024,1024]{1,0:T(8,128)} %get-tuple-element.9.so_far, f32[256,1024]{1,0:T(8,128)} %get-tuple-element.10.weights, f32[2,256,512]{2,1,0:T(8,128)} %get-tuple-element.11.slab), custom_call_target="tpu_custom_call" | custom-call | tf_op jit(solution)/shard_map/pallas_call | solution.py:745
  126.6 0.0 copy-done.1
  126.6 0.6 copy.9
  127.2 0.0 copy-done
  127.2 0.8 copy.10
Async XLA Ops:
  119.9 6.7 %copy-start.1 = (f32[1,1024]{1,0:T(1,128)S(1)}, f32[1,1024]{1,0:T(1,128)}, u32[]{:S(2)}) copy-start(f32[1,1024]{1,0:T(1,128)} %get-tuple-element.8) | copy-start | bytes 12292
  119.9 7.3 %copy-start = (f32[256,512]{1,0:T(8,128)S(1)}, f32[256,512]{1,0:T(8,128)}, u32[]{:S(2)}) copy-start(f32[256,512]{1,0:T(8,128)} %get-tuple-element.18) | copy-start | bytes 1572868
